TPU v7x, 32 devices: a whole 2x2x4 slice. The times are simulated.
32 devices in a mesh: grp: 2 (over x), req: 16 (over z, y, core).
Axes of the slice: x: 2, y: 2, z: 4, core: 2. Of those that a mesh axis runs over, the one named last changes fastest.
Arguments:
- xbc: bfloat16 [4096, 9216], P(('grp', 'req')), parts along dimension 0, may hold values from -6 to 6
- dt_raw: float32 [4096, 128], P(('grp', 'req')), parts along dimension 0, may hold values from -6 to 6
- conv_weight: float32 [4, 9216], replicated, may hold values from -3 to 3
- conv_bias: float32 [9216], replicated, may hold values from -3 to 3
- dt_bias: float32 [128], replicated, may hold values from -1 to 1
- a_log: float32 [128], replicated, may hold values from -6 to -2.5
- d_skip: float32 [128], replicated, may hold values from 0.5 to 1.5
- cache_states: bfloat16 [96, 128, 8192], P(('grp', 'req')), parts along dimension 0, may hold values from -24 to 24
- cache_tails: bfloat16 [96, 3, 9216], P(('grp', 'req')), parts along dimension 0, may hold values from -6 to 6
- hit_owner: int32 [32], P('grp'), parts along dimension 0, may hold values from 0 to 15, as said below
- hit_slot: int32 [32], P('grp'), parts along dimension 0, may hold values from 0 to 2, as said below
- hit_spans: int32 [32], P('grp'), parts along dimension 0, may hold values from 0 to 4
- request_of: int32 [32], P(('grp', 'req')), parts along dimension 0, may hold values from 0 to 15, each once
Outputs:
- y_out: bfloat16 [4096, 8192], P(('grp', 'req')), parts along dimension 0
- final_state: bfloat16 [32, 128, 8192], P(('grp', 'req')), parts along dimension 0
There are 2 independent parts, one for each index of `grp`. A program takes and returns all parts, laid end to end along the dimension named above; an argument that names none is the same for every part. Nothing has to cross between parts.
Inputs may be any that keep to these rules, and one draw needn't show every extreme that they name: `hit_owner`: owners are skewed: some devices hold the prefixes of several requests, others of none. `hit_slot`: all requests that name the same owner device name the same slot of it. `request_of`: each request stands on exactly one device.
All inputs are finite; a program needn't handle non-finite values.
Results may differ from a plain program's by a relative error of at most 0.0039.
Values may be sent and summed in bfloat16 or wider, within the bound.
No kernel may reach another device: no remote copies, remote signals or barrier semaphores. Data moves between devices by JAX's collectives and lax.ppermute only.
A program may use at most 128 MiB of HBM per device.

v0:
```python
import functools

import jax
import jax.numpy as jnp
from jax import lax
from jax.experimental import pallas as pl
from jax.experimental.pallas import tpu as pltpu
from jax.sharding import PartitionSpec as P

HEADS = 128
HEAD_DIM = 64
GROUPS = 4
NST = 128
INNER = 8192
SPAN = 128
PER_GROUP = HEADS // GROUPS
CHUNK = 512
CHUNK_HEADS = CHUNK // HEAD_DIM
CHUNKS = INNER // CHUNK
GROUP_CHUNKS = CHUNKS // GROUPS
CHANNELS = INNER + 2 * GROUPS * NST
EARLY = 3
GROUP = INNER // GROUPS
NOTE = 8
SMALL = pl.CostEstimate(flops=1000, bytes_accessed=1000, transcendentals=0)


def served_slot(device, owner_ref, slot_ref):
    served = jnp.int32(0)
    for r in range(owner_ref.shape[0]):
        served = jnp.where(owner_ref[r] == device, jnp.maximum(served, slot_ref[r]), served)
    return served


def piece_shape(pieces):
    width = INNER // pieces
    split = 2 if width >= 256 else 1
    return split, width // split


def pack_kernel(
    device_ref, owner_ref, slot_ref, request_ref, cache_ref, tails_ref, held, tail, note, sems_in, sem
):
    pieces = held.shape[0]
    split, width = piece_shape(pieces)
    share = (CHANNELS - INNER) // pieces
    served = served_slot(device_ref[0], owner_ref, slot_ref)
    tail_copy = pltpu.make_async_copy(tails_ref.at[served], tail, sem)
    tail_copy.start()
    into = []
    for p in range(pieces):
        for k in range(split):
            source = cache_ref.at[served, :, pl.ds((p * split + k) * width, width)]
            into.append(pltpu.make_async_copy(source, held.at[p, pl.ds(k * NST, NST)], sems_in.at[p, k]))
    for copy in into:
        copy.start()
    note[...] = jnp.zeros(note.shape, jnp.float32)
    note[7:8, :] = jnp.full((1, width), owner_ref[request_ref[0]].astype(jnp.float32))
    tail_copy.wait()
    last = tail[...].astype(jnp.float32)
    taps = last.shape[0]
    for p in range(pieces):
        for k in range(split):
            first = (p * split + k) * width
            note[k * taps : (k + 1) * taps, :] = last[:, first : first + width]
        first = INNER + p * share
        for r in range(taps):
            note[6:7, r * share : (r + 1) * share] = last[r : r + 1, first : first + share]
        held[p, split * NST :, :] = note[...].astype(jnp.bfloat16)
    for copy in into:
        copy.wait()


def pack(device, hit_owner, hit_slot, request_of, cache_states, cache_tails, pieces):
    smem = pl.BlockSpec(memory_space=pltpu.SMEM)
    hbm = pl.BlockSpec(memory_space=pl.ANY)
    split, width = piece_shape(pieces)
    shape = (pieces, split * NST + NOTE, width)
    return pl.pallas_call(
        pack_kernel,
        out_shape=pltpu.VMEM(shape, jnp.bfloat16),
        in_specs=[smem] * 4 + [hbm, hbm],
        out_specs=pl.BlockSpec(memory_space=pltpu.VMEM),
        scratch_shapes=[
            pltpu.VMEM(cache_tails.shape[1:], jnp.bfloat16),
            pltpu.VMEM((NOTE, width), jnp.float32),
            pltpu.SemaphoreType.DMA((pieces, split)),
            pltpu.SemaphoreType.DMA,
        ],
        compiler_params=pltpu.CompilerParams(vmem_limit_bytes=56 * 1024 * 1024),
        cost_estimate=SMALL,
        name="pack",
    )(device, hit_owner, hit_slot, request_of, cache_states, cache_tails)


def choose_kernel(held, out_ref, sems_out):
    pieces, rows, _ = held.shape
    wanted = []
    for p in range(pieces):
        wanted.append(jnp.max(held[p, rows - NOTE :, :128].astype(jnp.float32)[7:8]).astype(jnp.int32))
    outof = []
    for p in range(pieces):
        outof.append(pltpu.make_async_copy(held.at[wanted[p]], out_ref.at[p], sems_out.at[p]))
        outof[p].start()
    for copy in outof:
        copy.wait()


def choose(parts):
    pieces = parts.shape[0]
    hbm = pl.BlockSpec(memory_space=pl.ANY)
    return pl.pallas_call(
        choose_kernel,
        out_shape=jax.ShapeDtypeStruct(parts.shape, jnp.bfloat16),
        in_specs=[pl.BlockSpec(memory_space=pltpu.VMEM)],
        out_specs=hbm,
        scratch_shapes=[
            pltpu.SemaphoreType.DMA((pieces,)),
        ],
        compiler_params=pltpu.CompilerParams(vmem_limit_bytes=16 * 1024 * 1024),
        cost_estimate=SMALL,
        name="choose",
    )(parts)


def convolved(extended, weight, bias):
    total = bias + weight[3:4, :] * extended
    for back in range(1, 4):
        total = total + weight[3 - back : 4 - back, :] * pltpu.roll(extended, back, 0)
    return total / (1.0 + jnp.exp(-total))


def local_kernel(
    x_ref, xb_ref, xc_ref, w_ref, wb_ref, wc_ref, b_ref, bb_ref, bc_ref,
    dt_ref, dt_bias_ref, a_log_ref, skip_ref,
    y_ref, fresh_ref, c_out_ref, growth_ref, early_ref, early_carry_ref,
    cum_cols, step_cols, cum_rows, step_rows, carry_cols, scores, b_state,
):
    i = pl.program_id(0)
    rows = SPAN
    t_of = lax.broadcasted_iota(jnp.int32, (rows, rows), 0)
    s_of = lax.broadcasted_iota(jnp.int32, (rows, rows), 1)

    @pl.when(pl.program_id(0) == 0)
    def _():
        v = dt_ref[...] + dt_bias_ref[...]
        step = jnp.maximum(v, 0.0) + jnp.log1p(jnp.exp(-jnp.abs(v)))
        rate = -jnp.exp(a_log_ref[...])
        cum = step * rate
        shift = 1
        while shift < rows:
            cum = cum + jnp.where(t_of >= shift, pltpu.roll(cum, shift, 0), 0.0)
            shift *= 2
        growth_ref[...] = jnp.exp(cum)
        carry = jnp.exp(cum[rows - 1 : rows, :] - cum) * step
        for c in range(CHUNKS):
            cum_cols[c] = cum[:, c * CHUNK_HEADS : (c + 1) * CHUNK_HEADS]
            step_cols[c] = step[:, c * CHUNK_HEADS : (c + 1) * CHUNK_HEADS]
            carry_cols[c] = carry[:, c * CHUNK_HEADS : (c + 1) * CHUNK_HEADS]
        cum_rows[...] = cum.T
        step_rows[...] = step.T

    @pl.when(i % GROUP_CHUNKS == 0)
    def _():
        b_part = convolved(xb_ref[...].astype(jnp.float32), wb_ref, bb_ref[...])
        b_part = jnp.where(t_of >= EARLY, b_part, 0.0).astype(jnp.bfloat16)
        c_part = convolved(xc_ref[...].astype(jnp.float32), wc_ref, bc_ref[...]).astype(jnp.bfloat16)
        b_state[...] = b_part
        c_out_ref[...] = c_part
        both = lax.dot_general(c_part, b_part, (((1,), (1,)), ((), ())), preferred_element_type=jnp.float32)
        scores[...] = jnp.where(t_of >= s_of, both, 0.0)

    x = convolved(x_ref[...].astype(jnp.float32), w_ref, b_ref[...])
    x = jnp.where(lax.broadcasted_iota(jnp.int32, x.shape, 0) >= EARLY, x, 0.0).astype(jnp.bfloat16)
    x32 = x.astype(jnp.float32)
    first = pl.multiple_of(i * CHUNK_HEADS, CHUNK_HEADS)
    cum_r = cum_rows[pl.ds(first, CHUNK_HEADS), :]
    step_r = step_rows[pl.ds(first, CHUNK_HEADS), :]
    cum_c = cum_cols[i]
    carry_c = carry_cols[i]
    low = lax.broadcasted_iota(jnp.int32, (rows, 128), 1) < HEAD_DIM
    zero = jnp.zeros((rows, 128), jnp.bfloat16)
    step_c = step_cols[i]
    t_col = lax.broadcasted_iota(jnp.int32, (rows, CHUNK_HEADS), 0)
    early = []
    for s in range(EARLY):
        decay = jnp.exp(jnp.minimum(cum_c - cum_c[s : s + 1, :], 0.0)) * step_c[s : s + 1, :]
        early.append(jnp.where(t_col >= s, decay, 0.0))
    early = jnp.concatenate(early + [jnp.zeros((rows, CHUNK_HEADS), jnp.float32)], axis=1)
    for c in range(GROUP_CHUNKS):

        @pl.when(i % GROUP_CHUNKS == c)
        def _(c=c):
            early_ref[0, :, c * 4 * CHUNK_HEADS : (c + 1) * 4 * CHUNK_HEADS] = early

    for pair in range(CHUNK_HEADS // 2):
        mixes = []
        for j in (2 * pair, 2 * pair + 1):
            diff = cum_c[:, j : j + 1] - cum_r[j : j + 1, :]
            mixes.append((scores[...] * jnp.exp(jnp.minimum(diff, 0.0)) * step_r[j : j + 1, :]).astype(jnp.bfloat16))
        xp = x[:, pair * 128 : (pair + 1) * 128]
        stacked = jnp.concatenate([jnp.where(low, xp, zero), jnp.where(low, zero, xp)], axis=0)
        y = jnp.dot(jnp.concatenate(mixes, axis=1), stacked, preferred_element_type=jnp.float32)
        cols = slice(pair * 128, (pair + 1) * 128)
        y_ref[:, cols] = y + skip_ref[:, cols] * x32[:, cols]
        weight = jnp.where(low, carry_c[:, 2 * pair : 2 * pair + 1], carry_c[:, 2 * pair + 1 : 2 * pair + 2])
        early_carry_ref[:, cols] = weight[:8]
        carried = (weight * x32[:, cols]).astype(jnp.bfloat16)
        fresh_ref[:, cols] = lax.dot_general(
            b_state[...], carried, (((0,), (0,)), ((), ())), preferred_element_type=jnp.float32
        )


def local_part(xbc, conv_weight, conv_bias, dt_raw, dt_bias, a_log, skip):
    rows = xbc.shape[0]
    bias = conv_bias[None, :]
    first_b = INNER // 128

    def blocks(height):
        return [
            pl.BlockSpec((height, CHUNK), lambda i: (0, i)),
            pl.BlockSpec((height, 128), lambda i: (0, first_b + i // GROUP_CHUNKS)),
            pl.BlockSpec((height, 128), lambda i: (0, first_b + GROUPS + i // GROUP_CHUNKS)),
        ]

    whole = lambda *shape: pl.BlockSpec(shape, lambda i: (0, 0))
    return pl.pallas_call(
        local_kernel,
        grid=(CHUNKS,),
        out_shape=(
            pltpu.HBM((rows, INNER), jnp.float32),
            pltpu.HBM((NST, INNER), jnp.float32),
            pltpu.HBM((rows, GROUPS * NST), jnp.bfloat16),
            pltpu.HBM((rows, HEADS), jnp.float32),
            pltpu.HBM((GROUPS, rows, 128), jnp.float32),
            pltpu.HBM((8, INNER), jnp.float32),
        ),
        in_specs=blocks(rows) + blocks(4) + blocks(1)
        + [whole(rows, HEADS), whole(1, HEADS), whole(1, HEADS), pl.BlockSpec((1, CHUNK), lambda i: (0, i))],
        out_specs=(
            pl.BlockSpec((rows, CHUNK), lambda i: (0, i)),
            pl.BlockSpec((NST, CHUNK), lambda i: (0, i)),
            pl.BlockSpec((rows, NST), lambda i: (0, i // GROUP_CHUNKS)),
            whole(rows, HEADS),
            pl.BlockSpec((1, rows, 128), lambda i: (i // GROUP_CHUNKS, 0, 0)),
            pl.BlockSpec((8, CHUNK), lambda i: (0, i)),
        ),
        scratch_shapes=[
            pltpu.VMEM((CHUNKS, rows, CHUNK_HEADS), jnp.float32),
            pltpu.VMEM((CHUNKS, rows, CHUNK_HEADS), jnp.float32),
            pltpu.VMEM((HEADS, rows), jnp.float32),
            pltpu.VMEM((HEADS, rows), jnp.float32),
            pltpu.VMEM((CHUNKS, rows, CHUNK_HEADS), jnp.float32),
            pltpu.VMEM((rows, rows), jnp.float32),
            pltpu.VMEM((rows, NST), jnp.bfloat16),
        ],
        compiler_params=pltpu.CompilerParams(vmem_limit_bytes=24 * 1024 * 1024),
        cost_estimate=pl.CostEstimate(flops=1000, bytes_accessed=1000, transcendentals=0),
        name="local_part",
    )(
        xbc, xbc, xbc, conv_weight, conv_weight, conv_weight, bias, bias, bias,
        dt_raw, dt_bias[None, :], a_log[None, :], skip,
    )


def state_kernel(
    live_ref, start_ref, xbc_ref, c_hbm, growth_hbm, early_hbm, carry_hbm, w_hbm, bias_hbm, skip_hbm, y_ref, fresh_ref,
    y_out_ref, final_ref,
    raw, x_in, c_ref, growth_ref, early_ref, early_carry_ref, w_ref, bias_ref, skip_ref,
    y_in, fresh_in, y_done, final_done, tail, c_full, sems, sems_raw, sems_in, sems_out,
):
    pieces, height, width = raw.shape
    split = height // NST
    blocks = GROUP // width
    share = (CHANNELS - INNER) // pieces
    live = live_ref[0] > 0
    starts = [pltpu.make_async_copy(start_ref.at[p], raw.at[p], sems_raw.at[p]) for p in range(pieces)]
    small = (
        (xbc_ref.at[pl.ds(0, 16)], x_in), (w_hbm, w_ref), (bias_hbm, bias_ref), (c_hbm, c_ref), (growth_hbm, growth_ref),
        (early_hbm, early_ref), (carry_hbm, early_carry_ref), (skip_hbm, skip_ref),
    )
    small = [pltpu.make_async_copy(a, b, sems.at[n]) for n, (a, b) in enumerate(small)]
    into, outof = [], []
    for g in range(GROUPS):
        columns = pl.ds(g * GROUP, GROUP)
        into.append(
            (
                pltpu.make_async_copy(y_ref.at[:, columns], y_in.at[g], sems_in.at[g, 0]),
                pltpu.make_async_copy(fresh_ref.at[:, columns], fresh_in.at[g], sems_in.at[g, 1]),
            )
        )
        outof += [
            pltpu.make_async_copy(y_done.at[g], y_out_ref.at[:, columns], sems_out.at[g, 0]),
            pltpu.make_async_copy(final_done.at[g], final_ref.at[0, :, columns], sems_out.at[g, 1]),
        ]
    for copy in starts + small:
        copy.start()
    for copies in into:
        for copy in copies:
            copy.start()

    tail[...] = jnp.zeros(tail.shape, jnp.float32)
    for p in range(pieces):
        starts[p].wait()
        note = raw[p, split * NST :, :].astype(jnp.float32)
        note = jnp.where(live, note, 0.0)
        for k in range(split):
            first = (p * split + k) * width
            tail[5:8, first : first + width] = note[k * EARLY : (k + 1) * EARLY, :]
        first = INNER + p * share
        for r in range(EARLY):
            tail[5 + r : 6 + r, first : first + share] = note[6:7, r * share : (r + 1) * share]
    for copy in small:
        copy.wait()

    def early_rows(first, size):
        here = slice(first, first + size)
        extended = jnp.concatenate([tail[:, here], x_in[:, here].astype(jnp.float32)[:8]], axis=0)
        rows = convolved(extended, w_ref[:, here], bias_ref[:, here])[8:]
        rows = jnp.where(lax.broadcasted_iota(jnp.int32, rows.shape, 0) < EARLY, rows, 0.0)
        return rows.astype(jnp.bfloat16).astype(jnp.float32)

    def padded(rows):
        return jnp.concatenate([rows, jnp.zeros_like(rows)], axis=0).astype(jnp.bfloat16)

    b_early = early_rows(INNER, GROUPS * NST)
    c_early = padded(early_rows(INNER + GROUPS * NST, GROUPS * NST))
    c_full[...] = c_ref[...]
    sixteen = lax.broadcasted_iota(jnp.int32, c_early.shape, 0)
    c_full[:16, :] = jnp.where(sixteen < EARLY, c_early, c_ref[:16, :])

    grown = jnp.where(live, growth_ref[...], 0.0)
    group_head = lax.broadcasted_iota(jnp.int32, (4 * PER_GROUP, width), 0)
    lane_of = lax.broadcasted_iota(jnp.int32, (4 * PER_GROUP, width), 1) // HEAD_DIM
    spreads = []
    for n in range(blocks):
        mine = (group_head % PER_GROUP == lane_of + n * (width // HEAD_DIM)) & (group_head < 3 * PER_GROUP)
        spreads.append(jnp.where(mine, 1.0, 0.0).astype(jnp.bfloat16))
    row = lax.broadcasted_iota(jnp.int32, (128, 128), 0)
    token = row % (4 * CHUNK_HEADS) // CHUNK_HEADS
    own_head = lax.broadcasted_iota(jnp.int32, (CHUNK_HEADS, width), 0)
    lane_head = lax.broadcasted_iota(jnp.int32, (CHUNK_HEADS, width), 1) // HEAD_DIM

    def by_token(of, rows):
        return jnp.where(of == 0, rows[0:1], jnp.where(of == 1, rows[1:2], jnp.where(of == 2, rows[2:3], 0.0)))

    for g in range(GROUPS):
        c_group = c_full[:, g * NST : (g + 1) * NST]
        b_group = b_early[:, g * NST : (g + 1) * NST]
        both = lax.dot_general(
            c_group, by_token(token, b_group).astype(jnp.bfloat16), (((1,), (1,)), ((), ())),
            preferred_element_type=jnp.float32,
        )
        mixing = (both * early_ref[g]).astype(jnp.bfloat16)
        b_group = padded(b_group)
        rest = grown[:, g * PER_GROUP : (g + 1) * PER_GROUP]
        exact = []
        for _ in range(3):
            exact.append(rest.astype(jnp.bfloat16).astype(jnp.float32))
            rest = rest - exact[-1]
        exact = jnp.concatenate(exact + [jnp.zeros_like(rest)], axis=1).astype(jnp.bfloat16)
        for copy in into[g]:
            copy.wait()
        for n in range(blocks):
            first = g * GROUP + n * width
            here, inside = slice(first, first + width), slice(n * width, (n + 1) * width)
            x_early = early_rows(first, width)
            base = first // width % split * NST
            start = raw[first // (split * width), base : base + NST, :]
            y_state = jnp.dot(c_group, start, preferred_element_type=jnp.float32)
            growth = jnp.dot(exact, spreads[n], preferred_element_type=jnp.float32)
            chunk = n * width // CHUNK
            mine = own_head == lane_head + n * width % CHUNK // HEAD_DIM
            inputs = [jnp.where(mine, x_early[s : s + 1], 0.0) for s in range(EARLY)]
            inputs = jnp.concatenate(inputs + [jnp.zeros_like(inputs[0])], axis=0).astype(jnp.bfloat16)
            factors = mixing[:, chunk * 4 * CHUNK_HEADS : (chunk + 1) * 4 * CHUNK_HEADS]
            y = y_in[g, :, inside] + growth * y_state + jnp.dot(factors, inputs, preferred_element_type=jnp.float32)
            skipped = y[:8] + skip_ref[:, here] * x_early
            y_done[g, :, inside] = jnp.concatenate([skipped, y[8:]], axis=0).astype(jnp.bfloat16)
            carried = padded(early_carry_ref[:, here] * x_early)
            fresh = fresh_in[g, :, inside] + lax.dot_general(
                b_group, carried, (((0,), (0,)), ((), ())), preferred_element_type=jnp.float32
            )
            kept = growth[SPAN - 1 :, :] * start.astype(jnp.float32)
            final_done[g, :, inside] = (kept + fresh).astype(jnp.bfloat16)
        outof[2 * g].start()
        outof[2 * g + 1].start()
    for copy in outof:
        copy.wait()


def state_part(live, start, xbc, local_results, conv_weight, conv_bias, skip):
    y_local, fresh, c_part, growth, early, early_carry = local_results
    rows = y_local.shape[0]
    hbm = pl.BlockSpec(memory_space=pl.ANY)
    return pl.pallas_call(
        state_kernel,
        out_shape=(
            jax.ShapeDtypeStruct((rows, INNER), jnp.bfloat16),
            jax.ShapeDtypeStruct((1, NST, INNER), jnp.bfloat16),
        ),
        in_specs=[pl.BlockSpec(memory_space=pltpu.SMEM)] + [hbm] * 11,
        out_specs=(hbm, hbm),
        scratch_shapes=[
            pltpu.VMEM(start.shape, jnp.bfloat16),
            pltpu.VMEM((16, CHANNELS), jnp.bfloat16),
            pltpu.VMEM(c_part.shape, c_part.dtype),
            pltpu.VMEM(growth.shape, growth.dtype),
            pltpu.VMEM(early.shape, early.dtype),
            pltpu.VMEM(early_carry.shape, early_carry.dtype),
            pltpu.VMEM(conv_weight.shape, conv_weight.dtype),
            pltpu.VMEM((1, CHANNELS), jnp.float32),
            pltpu.VMEM((1, INNER), jnp.float32),
            pltpu.VMEM((GROUPS, rows, GROUP), jnp.float32),
            pltpu.VMEM((GROUPS, NST, GROUP), jnp.float32),
            pltpu.VMEM((GROUPS, rows, GROUP), jnp.bfloat16),
            pltpu.VMEM((GROUPS, NST, GROUP), jnp.bfloat16),
            pltpu.VMEM((8, CHANNELS), jnp.float32),
            pltpu.VMEM((rows, GROUPS * NST), jnp.bfloat16),
            pltpu.SemaphoreType.DMA((8,)),
            pltpu.SemaphoreType.DMA((start.shape[0],)),
            pltpu.SemaphoreType.DMA((GROUPS, 2)),
            pltpu.SemaphoreType.DMA((GROUPS, 2)),
        ],
        compiler_params=pltpu.CompilerParams(vmem_limit_bytes=52 * 1024 * 1024),
        cost_estimate=pl.CostEstimate(flops=3 * 134_000_000, bytes_accessed=15_000_000, transcendentals=0),
        name="state_part",
    )(live, start, xbc, c_part, growth, early, early_carry, conv_weight, conv_bias[None, :], skip, y_local, fresh)


def local(
    xbc, dt_raw, conv_weight, conv_bias, dt_bias, a_log, d_skip, cache_states, cache_tails,
    hit_owner, hit_slot, hit_spans, request_of,
):
    pieces = hit_owner.shape[0]
    place = lax.axis_index("req").astype(jnp.int32)[None]
    packed = pack(place, hit_owner, hit_slot, request_of, cache_states, cache_tails, pieces)
    parts = lax.all_to_all(packed, "req", split_axis=0, concat_axis=0, tiled=True)
    skip = jnp.repeat(d_skip, HEAD_DIM)[None, :]
    without = local_part(xbc, conv_weight, conv_bias, dt_raw, dt_bias, a_log, skip)
    parts, without = lax.optimization_barrier((parts, without))
    start = lax.all_to_all(choose(parts), "req", split_axis=0, concat_axis=0, tiled=True)

    live = (hit_spans[request_of[0]] > 0).astype(jnp.int32)[None]
    return state_part(live, start, xbc, without, conv_weight, conv_bias, skip)


def solution(mesh):
    in_specs = (
        P(("grp", "req"), None),
        P(("grp", "req"), None),
        P(),
        P(),
        P(),
        P(),
        P(),
        P(("grp", "req"), None, None),
        P(("grp", "req"), None, None),
        P("grp"),
        P("grp"),
        P("grp"),
        P(("grp", "req")),
    )
    out_specs = (P(("grp", "req"), None), P(("grp", "req"), None, None))
    return jax.shard_map(local, mesh=mesh, in_specs=in_specs, out_specs=out_specs, check_vma=False)
```

profile of v0, /device:TPU:15, one launch (start us, length us, event | category | flops | bytes accessed | tf_op | source)
XLA Modules:
  0.0 125.4 jit_solution(2500993218265701843)
XLA Ops:
  1.3 2.9 %pack.1 = bf16[16,264,256]{2,1,0:T(8,128)(2,1)S(1)} custom-call(s32[1]{0:T(128)} %bitcast.1.device_ref, s32[16]{0:T(128)} %owner_ref.1, s32[16]{0:T(128)} %slot_ref.1, s32[1]{0:T(128)} %copy.15.request_ref, bf16[3,128,8192]{2,1,0:T(8,128)(2,1)} %cache_ref.1, bf16[3,3,9216]{2,1,0:T(4,128)(2,1)} %tails_ref.1), custom_call_target="tpu_custom_call" | custom-call | flops 1000 | bytes 1000 | tf_op jit(solution)/shard_map/pack/pallas_call | solution.py:79
  4.2 0.0 copy-start.1
  4.2 1.4 %copy-done.1 = bf16[16,264,256]{2,1,0:T(8,128)(2,1)} copy-done((bf16[16,264,256]{2,1,0:T(8,128)(2,1)}, bf16[16,264,256]{2,1,0:T(8,128)(2,1)S(1)}, u32[]{:S(2)}) %copy-start.1) | copy-done | bytes 2162712
  5.6 0.0 copy-start.7
  5.6 0.0 copy-start.9
  5.6 0.0 copy-start.10
  5.6 6.8 %all-to-all-start = ((bf16[16,264,256]{2,1,0:T(8,128)(2,1)}), bf16[16,264,256]{2,1,0:T(8,128)(2,1)}, u32[]{:S(2)}, u32[]{:S(2)}) async-start(bf16[16,264,256]{2,1,0:T(8,128)(2,1)} %copy-done.1), calls=%async_computation | async-start | bytes 4325376 | tf_op jit(solution)/shard_map/all_to_all | solution.py:438
  12.4 0.0 copy-done.11
  12.4 0.1 broadcast_in_dim.21
  12.5 0.1 broadcast_in_dim_reshape.3.skip_ref.skip_hbm
  12.6 0.0 copy-done
  12.7 19.4 %local_part.1 = (f32[128,8192]{1,0:T(8,128)}, f32[128,8192]{1,0:T(8,128)}, bf16[128,512]{1,0:T(8,128)(2,1)}, f32[128,128]{1,0:T(8,128)}, f32[4,128,128]{2,1,0:T(8,128)}, /*index=5*/f32[8,8192]{1,0:T(8,128)}) custom-call(bf16[128,9216]{1,0:T(8,128)(2,1)S(1)} %copy-done, bf16[128,9216]{1,0:T(8,128)(2,1)S(1)} %copy-done, bf16[128,9216]{1,0:T(8,128)(2,1)S(1)} %copy-done, ...), custom_call_target="tpu_custom_call" | custom-call | flops 1000 | bytes 1000 | tf_op jit(solution)/shard_map/local_part/pallas_call | solution.py:227
  32.1 29.3 %all-to-all-done.held = bf16[16,264,256]{2,1,0:T(8,128)(2,1)} async-done(((bf16[16,264,256]{2,1,0:T(8,128)(2,1)}), bf16[16,264,256]{2,1,0:T(8,128)(2,1)}, u32[]{:S(2)}, u32[]{:S(2)}) %all-to-all-start) | async-done | bytes 2162720 | tf_op jit(solution)/shard_map/all_to_all | solution.py:438
  61.4 3.2 %choose.1 = bf16[16,264,256]{2,1,0:T(8,128)(2,1)} custom-call(bf16[16,264,256]{2,1,0:T(8,128)(2,1)} %all-to-all-done.held), custom_call_target="tpu_custom_call" | custom-call | flops 1000 | bytes 1000 | tf_op jit(solution)/shard_map/choose/pallas_call | solution.py:112
  64.6 0.0 copy-start.12
  64.6 0.0 copy-start.4
  64.6 0.0 copy-start.5
  64.6 0.0 copy-start.6
  64.7 0.0 copy-start.8
  64.7 5.1 %all-to-all-start.1 = ((bf16[16,264,256]{2,1,0:T(8,128)(2,1)}), bf16[16,264,256]{2,1,0:T(8,128)(2,1)}, u32[]{:S(2)}, u32[]{:S(2)}) async-start(bf16[16,264,256]{2,1,0:T(8,128)(2,1)} %choose.1), calls=%async_computation.1 | async-start | bytes 4325376 | tf_op jit(solution)/shard_map/all_to_all | solution.py:442
  69.7 0.6 dynamic_slice.3
  71.0 47.6 %all-to-all-done.1.start_ref = bf16[16,264,256]{2,1,0:T(8,128)(2,1)} async-done(((bf16[16,264,256]{2,1,0:T(8,128)(2,1)}), bf16[16,264,256]{2,1,0:T(8,128)(2,1)}, u32[]{:S(2)}, u32[]{:S(2)}) %all-to-all-start.1) | async-done | bytes 2162720 | tf_op jit(solution)/shard_map/all_to_all | solution.py:442
  118.7 0.0 copy-done.8
  118.7 6.7 %state_part.1 = (bf16[128,8192]{1,0:T(8,128)(2,1)}, bf16[1,128,8192]{2,1,0:T(8,128)(2,1)}) custom-call(s32[1]{0:T(128)S(6)} %convert_element_type.4.live_ref, bf16[16,264,256]{2,1,0:T(8,128)(2,1)} %all-to-all-done.1.start_ref, bf16[128,9216]{1,0:T(8,128)(2,1)} %xbc_ref.1, bf16[128,512]{1,0:T(8,128)(2,1)S(1)} %copy-done.6, f32[128,128]{1,0:T(8,128)S(1)} %copy-done.8, ...), custom_call_target="tpu_custom_call" | custom-call | flops 402000000 | bytes 15000000 | tf_op jit(solution)/shard_map/state_part/pallas_call | solution.py:396
  (13 shorter events, 0.0 us)
Async XLA Ops:
  4.2 1.4 %copy-start.1 = (bf16[16,264,256]{2,1,0:T(8,128)(2,1)}, bf16[16,264,256]{2,1,0:T(8,128)(2,1)S(1)}, u32[]{:S(2)}) copy-start(bf16[16,264,256]{2,1,0:T(8,128)(2,1)S(1)} %pack.1) | copy-start | bytes 6488068
  5.6 6.9 %copy-start.11 = (f32[128]{0:T(128)S(1)}, f32[128]{0:T(128)}, u32[]{:S(2)}) copy-start(f32[128]{0:T(128)} %param.19) | copy-start | bytes 1540
  5.6 7.1 %copy-start = (bf16[128,9216]{1,0:T(8,128)(2,1)S(1)}, bf16[128,9216]{1,0:T(8,128)(2,1)}, u32[]{:S(2)}) copy-start(bf16[128,9216]{1,0:T(8,128)(2,1)} %xbc_ref.1) | copy-start | bytes 7077892
  5.6 7.1 %copy-start.2 = (f32[4,9216]{1,0:T(4,128)S(1)}, f32[4,9216]{1,0:T(4,128)}, u32[]{:S(2)}) copy-start(f32[4,9216]{1,0:T(4,128)} %w_hbm.1) | copy-start | bytes 442372
  5.6 7.1 %copy-start.3 = (f32[9216]{0:T(1024)S(1)}, f32[9216]{0:T(1024)}, u32[]{:S(2)}) copy-start(f32[9216]{0:T(1024)} %param.16) | copy-start | bytes 110596
  5.6 7.1 %copy-start.7 = (f32[128,128]{1,0:T(8,128)S(1)}, f32[128,128]{1,0:T(8,128)}, u32[]{:S(2)}) copy-start(f32[128,128]{1,0:T(8,128)} %dt_ref.1) | copy-start | bytes 196612
  5.6 7.1 %copy-start.9 = (f32[128]{0:T(128)S(1)}, f32[128]{0:T(128)}, u32[]{:S(2)}) copy-start(f32[128]{0:T(128)} %param.17) | copy-start | bytes 1540
  5.6 7.1 %copy-start.10 = (f32[128]{0:T(128)S(1)}, f32[128]{0:T(128)}, u32[]{:S(2)}) copy-start(f32[128]{0:T(128)} %param.18) | copy-start | bytes 1540
  5.6 55.8 %all-to-all-start = ((bf16[16,264,256]{2,1,0:T(8,128)(2,1)}), bf16[16,264,256]{2,1,0:T(8,128)(2,1)}, u32[]{:S(2)}, u32[]{:S(2)}) async-start(bf16[16,264,256]{2,1,0:T(8,128)(2,1)} %copy-done.1), calls=%async_computation | async-start | bytes 4325376 | tf_op jit(solution)/shard_map/all_to_all | solution.py:438
  64.6 5.1 %copy-start.12 = (s32[16]{0:T(128)S(1)}, s32[16]{0:T(128)}, u32[]{:S(2)}) copy-start(s32[16]{0:T(128)} %param.24) | copy-start | bytes 196
  64.6 54.0 %copy-start.4 = (f32[4,128,128]{2,1,0:T(8,128)S(1)}, f32[4,128,128]{2,1,0:T(8,128)}, u32[]{:S(2)}) copy-start(f32[4,128,128]{2,1,0:T(8,128)} %get-tuple-element.24.early_hbm) | copy-start | bytes 786436
  64.6 54.0 %copy-start.5 = (f32[8,8192]{1,0:T(8,128)S(1)}, f32[8,8192]{1,0:T(8,128)}, u32[]{:S(2)}) copy-start(f32[8,8192]{1,0:T(8,128)} %get-tuple-element.25.carry_hbm) | copy-start | bytes 786436
  64.6 54.0 %copy-start.6 = (bf16[128,512]{1,0:T(8,128)(2,1)S(1)}, bf16[128,512]{1,0:T(8,128)(2,1)}, u32[]{:S(2)}) copy-start(bf16[128,512]{1,0:T(8,128)(2,1)} %get-tuple-element.22.c_hbm) | copy-start | bytes 393220
  64.7 54.0 %copy-start.8 = (f32[128,128]{1,0:T(8,128)S(1)}, f32[128,128]{1,0:T(8,128)}, u32[]{:S(2)}) copy-start(f32[128,128]{1,0:T(8,128)} %get-tuple-element.23.growth_hbm) | copy-start | bytes 196612
  64.7 54.0 %all-to-all-start.1 = ((bf16[16,264,256]{2,1,0:T(8,128)(2,1)}), bf16[16,264,256]{2,1,0:T(8,128)(2,1)}, u32[]{:S(2)}, u32[]{:S(2)}) async-start(bf16[16,264,256]{2,1,0:T(8,128)(2,1)} %choose.1), calls=%async_computation.1 | async-start | bytes 4325376 | tf_op jit(solution)/shard_map/all_to_all | solution.py:442
where the time goes:
time: 126 us; the launch traced here: 125 us
  waiting for transfers between devices  76.9 us (61%)
  Pallas kernels  32.3 us (26%)
  starting transfers between devices  11.9 us (9%)
  local copies, waits for them, and re-layouts  2.25 us (2%)
  between operations  2.08 us (2%)
    all_to_all x1, waiting for transfers between devices, local(): lax.all_to_all(choose(parts), 'req', split_axis=0, concat_axis=0, tiled=T...  47.6 us
    all_to_all x1, waiting for transfers between devices, local(): lax.all_to_all(packed, 'req', split_axis=0, concat_axis=0, tiled=True)  29.3 us
    pallas_call x1, Pallas kernels, local_part(): pl.pallas_call(local_kernel, grid=(CHUNKS,), out_shape=(pltpu.HBM((rows,...  19.4 us
    all_to_all x1, starting transfers between devices, local(): lax.all_to_all(packed, 'req', split_axis=0, concat_axis=0, tiled=True)  6.83 us
    pallas_call x1, Pallas kernels, state_part(): pl.pallas_call(state_kernel, out_shape=(jax.ShapeDtypeStruct((rows, INNER...  6.75 us
    all_to_all x1, starting transfers between devices, local(): lax.all_to_all(choose(parts), 'req', split_axis=0, concat_axis=0, tiled=T...  5.05 us
    pallas_call x1, Pallas kernels, choose(): pl.pallas_call(choose_kernel, out_shape=jax.ShapeDtypeStruct(parts.shape,...  3.24 us
    pallas_call x1, Pallas kernels, pack(): pl.pallas_call(pack_kernel, out_shape=pltpu.VMEM(shape, jnp.bfloat16), in...  2.9 us
  transfers between devices with their start and end apart: 2, of which 2 were waited for; matrix products, arithmetic and copies ran while one was open for 1% of the time, Pallas kernels for 15%

commit v1 on v0

--- a/solution.py
+++ b/solution.py
@@ -254,7 +254,7 @@
             pltpu.VMEM((rows, rows), jnp.float32),
             pltpu.VMEM((rows, NST), jnp.bfloat16),
         ],
-        compiler_params=pltpu.CompilerParams(vmem_limit_bytes=24 * 1024 * 1024),
+        compiler_params=pltpu.CompilerParams(vmem_limit_bytes=60 * 1024 * 1024),
         cost_estimate=pl.CostEstimate(flops=1000, bytes_accessed=1000, transcendentals=0),
         name="local_part",
     )(
@@ -264,9 +264,9 @@
 
 
 def state_kernel(
-    live_ref, start_ref, xbc_ref, c_hbm, growth_hbm, early_hbm, carry_hbm, w_hbm, bias_hbm, skip_hbm, y_ref, fresh_ref,
+    live_ref, start_ref, xbc_ref, c_hbm, growth_hbm, early_hbm, carry_hbm, channel_hbm, y_ref, fresh_ref,
     y_out_ref, final_ref,
-    raw, x_in, c_ref, growth_ref, early_ref, early_carry_ref, w_ref, bias_ref, skip_ref,
+    raw, x_in, c_ref, growth_ref, early_ref, early_carry_ref, channel_ref,
     y_in, fresh_in, y_done, final_done, tail, c_full, sems, sems_raw, sems_in, sems_out,
 ):
     pieces, height, width = raw.shape
@@ -276,8 +276,8 @@
     live = live_ref[0] > 0
     starts = [pltpu.make_async_copy(start_ref.at[p], raw.at[p], sems_raw.at[p]) for p in range(pieces)]
     small = (
-        (xbc_ref.at[pl.ds(0, 16)], x_in), (w_hbm, w_ref), (bias_hbm, bias_ref), (c_hbm, c_ref), (growth_hbm, growth_ref),
-        (early_hbm, early_ref), (carry_hbm, early_carry_ref), (skip_hbm, skip_ref),
+        (xbc_ref.at[pl.ds(0, 16)], x_in), (channel_hbm, channel_ref), (c_hbm, c_ref), (growth_hbm, growth_ref),
+        (early_hbm, early_ref), (carry_hbm, early_carry_ref),
     )
     small = [pltpu.make_async_copy(a, b, sems.at[n]) for n, (a, b) in enumerate(small)]
     into, outof = [], []
@@ -293,15 +293,18 @@
             pltpu.make_async_copy(y_done.at[g], y_out_ref.at[:, columns], sems_out.at[g, 0]),
             pltpu.make_async_copy(final_done.at[g], final_ref.at[0, :, columns], sems_out.at[g, 1]),
         ]
-    for copy in starts + small:
+    for copy in small + starts:
         copy.start()
-    for copies in into:
+    for copies in into[:2]:
         for copy in copies:
             copy.start()
-
     tail[...] = jnp.zeros(tail.shape, jnp.float32)
+    for copy in starts:
+        copy.wait()
+    for copies in into[2:]:
+        for copy in copies:
+            copy.start()
     for p in range(pieces):
-        starts[p].wait()
         note = raw[p, split * NST :, :].astype(jnp.float32)
         note = jnp.where(live, note, 0.0)
         for k in range(split):
@@ -316,7 +319,7 @@
     def early_rows(first, size):
         here = slice(first, first + size)
         extended = jnp.concatenate([tail[:, here], x_in[:, here].astype(jnp.float32)[:8]], axis=0)
-        rows = convolved(extended, w_ref[:, here], bias_ref[:, here])[8:]
+        rows = convolved(extended, channel_ref[:4, here], channel_ref[4:5, here])[8:]
         rows = jnp.where(lax.broadcasted_iota(jnp.int32, rows.shape, 0) < EARLY, rows, 0.0)
         return rows.astype(jnp.bfloat16).astype(jnp.float32)
 
@@ -375,7 +378,7 @@
             inputs = jnp.concatenate(inputs + [jnp.zeros_like(inputs[0])], axis=0).astype(jnp.bfloat16)
             factors = mixing[:, chunk * 4 * CHUNK_HEADS : (chunk + 1) * 4 * CHUNK_HEADS]
             y = y_in[g, :, inside] + growth * y_state + jnp.dot(factors, inputs, preferred_element_type=jnp.float32)
-            skipped = y[:8] + skip_ref[:, here] * x_early
+            skipped = y[:8] + channel_ref[5:6, here] * x_early
             y_done[g, :, inside] = jnp.concatenate([skipped, y[8:]], axis=0).astype(jnp.bfloat16)
             carried = padded(early_carry_ref[:, here] * x_early)
             fresh = fresh_in[g, :, inside] + lax.dot_general(
@@ -389,7 +392,7 @@
         copy.wait()
 
 
-def state_part(live, start, xbc, local_results, conv_weight, conv_bias, skip):
+def state_part(live, start, xbc, local_results, channels):
     y_local, fresh, c_part, growth, early, early_carry = local_results
     rows = y_local.shape[0]
     hbm = pl.BlockSpec(memory_space=pl.ANY)
@@ -399,7 +402,7 @@
             jax.ShapeDtypeStruct((rows, INNER), jnp.bfloat16),
             jax.ShapeDtypeStruct((1, NST, INNER), jnp.bfloat16),
         ),
-        in_specs=[pl.BlockSpec(memory_space=pltpu.SMEM)] + [hbm] * 11,
+        in_specs=[pl.BlockSpec(memory_space=pltpu.SMEM)] + [hbm] * 9,
         out_specs=(hbm, hbm),
         scratch_shapes=[
             pltpu.VMEM(start.shape, jnp.bfloat16),
@@ -408,24 +411,22 @@
             pltpu.VMEM(growth.shape, growth.dtype),
             pltpu.VMEM(early.shape, early.dtype),
             pltpu.VMEM(early_carry.shape, early_carry.dtype),
-            pltpu.VMEM(conv_weight.shape, conv_weight.dtype),
-            pltpu.VMEM((1, CHANNELS), jnp.float32),
-            pltpu.VMEM((1, INNER), jnp.float32),
+            pltpu.VMEM(channels.shape, channels.dtype),
             pltpu.VMEM((GROUPS, rows, GROUP), jnp.float32),
             pltpu.VMEM((GROUPS, NST, GROUP), jnp.float32),
             pltpu.VMEM((GROUPS, rows, GROUP), jnp.bfloat16),
             pltpu.VMEM((GROUPS, NST, GROUP), jnp.bfloat16),
             pltpu.VMEM((8, CHANNELS), jnp.float32),
             pltpu.VMEM((rows, GROUPS * NST), jnp.bfloat16),
-            pltpu.SemaphoreType.DMA((8,)),
+            pltpu.SemaphoreType.DMA((6,)),
             pltpu.SemaphoreType.DMA((start.shape[0],)),
             pltpu.SemaphoreType.DMA((GROUPS, 2)),
             pltpu.SemaphoreType.DMA((GROUPS, 2)),
         ],
-        compiler_params=pltpu.CompilerParams(vmem_limit_bytes=52 * 1024 * 1024),
+        compiler_params=pltpu.CompilerParams(vmem_limit_bytes=62 * 1024 * 1024),
         cost_estimate=pl.CostEstimate(flops=3 * 134_000_000, bytes_accessed=15_000_000, transcendentals=0),
         name="state_part",
-    )(live, start, xbc, c_part, growth, early, early_carry, conv_weight, conv_bias[None, :], skip, y_local, fresh)
+    )(live, start, xbc, c_part, growth, early, early_carry, channels, y_local, fresh)
 
 
 def local(
@@ -436,13 +437,13 @@
     place = lax.axis_index("req").astype(jnp.int32)[None]
     packed = pack(place, hit_owner, hit_slot, request_of, cache_states, cache_tails, pieces)
     parts = lax.all_to_all(packed, "req", split_axis=0, concat_axis=0, tiled=True)
+    start = lax.all_to_all(choose(parts), "req", split_axis=0, concat_axis=0, tiled=True)
+
+    live = (hit_spans[request_of[0]] > 0).astype(jnp.int32)[None]
     skip = jnp.repeat(d_skip, HEAD_DIM)[None, :]
     without = local_part(xbc, conv_weight, conv_bias, dt_raw, dt_bias, a_log, skip)
-    parts, without = lax.optimization_barrier((parts, without))
-    start = lax.all_to_all(choose(parts), "req", split_axis=0, concat_axis=0, tiled=True)
-
-    live = (hit_spans[request_of[0]] > 0).astype(jnp.int32)[None]
-    return state_part(live, start, xbc, without, conv_weight, conv_bias, skip)
+    channels = jnp.concatenate([conv_weight, conv_bias[None, :], jnp.pad(skip, ((0, 3), (0, CHANNELS - INNER)))], axis=0)
+    return state_part(live, start, xbc, without, channels)
 
 
 def solution(mesh):

time: 126 us -> 125 us (level)
  blocking collectives: 0 us -> 55.2 us
  waiting for transfers between devices: 76.9 us -> 24.9 us
  starting transfers between devices: 11.9 us -> 6.48 us
    all_to_all x0 -> x1, blocking collectives: none -> 55.2 us  [local(): lax.all_to_all(packed, 'req', split_axis=0, concat_axis=0, tiled=True)]
    all_to_all x1 -> x0, waiting for transfers between devices: 29.3 us -> none  [local(): lax.all_to_all(packed, 'req', split_axis=0, concat_axis=0, tiled=True)]
    all_to_all x1, waiting for transfers between devices: 47.6 us -> 24.9 us  [local(): lax.all_to_all(choose(parts), 'req', split_axis=0, concat_axis=0, tiled=T...]
    all_to_all x1 -> x0, starting transfers between devices: 6.83 us -> none  [local(): lax.all_to_all(packed, 'req', split_axis=0, concat_axis=0, tiled=True)]
    pallas_call x1, Pallas kernels: 3.24 us -> 1.61 us  [choose(): pl.pallas_call(choose_kernel, out_shape=jax.ShapeDtypeStruct(parts.shape,...]
    pallas_call x1, Pallas kernels: 19.4 us -> 20.9 us  [local_part(): pl.pallas_call(local_kernel, grid=(CHUNKS,), out_shape=(pltpu.HBM((rows,...]
    all_to_all x1, starting transfers between devices: 5.05 us -> 6.48 us  [local(): lax.all_to_all(choose(parts), 'req', split_axis=0, concat_axis=0, tiled=T...]
    unnamed x26 -> x10, local copies, waits for them, and re-layouts: 1.42 us -> 0.02 us
  transfers between devices with their start and end apart: 2 -> 1, of which waited for: 2 -> 1; matrix products, arithmetic and copies ran while one was open for 1% -> 2% of each run, Pallas kernels for 15% -> 17%
where the time goes in v1:
time: 125 us; the launch traced here: 124 us
  blocking collectives  55.2 us (44%)
  Pallas kernels  33.1 us (26%)
  waiting for transfers between devices  24.9 us (20%)
  starting transfers between devices  6.48 us (5%)
  between operations  2.01 us (2%)
  local copies, waits for them, and re-layouts  1.41 us (1%)
    all_to_all x1, blocking collectives, local(): lax.all_to_all(packed, 'req', split_axis=0, concat_axis=0, tiled=True)  55.2 us
    all_to_all x1, waiting for transfers between devices, local(): lax.all_to_all(choose(parts), 'req', split_axis=0, concat_axis=0, tiled=T...  24.9 us
    pallas_call x1, Pallas kernels, local_part(): pl.pallas_call(local_kernel, grid=(CHUNKS,), out_shape=(pltpu.HBM((rows,...  20.9 us
    pallas_call x1, Pallas kernels, state_part(): pl.pallas_call(state_kernel, out_shape=(jax.ShapeDtypeStruct((rows, INNER...  7.65 us
    all_to_all x1, starting transfers between devices, local(): lax.all_to_all(choose(parts), 'req', split_axis=0, concat_axis=0, tiled=T...  6.48 us
    pallas_call x1, Pallas kernels, pack(): pl.pallas_call(pack_kernel, out_shape=pltpu.VMEM(shape, jnp.bfloat16), in...  2.9 us
  transfers between devices with their start and end apart: 1, of which 1 were waited for; matrix products, arithmetic and copies ran while one was open for 2% of the time, Pallas kernels for 17%

profile of v1, /device:TPU:15, one launch (start us, length us, event | category | flops | bytes accessed | tf_op | source)
XLA Modules:
  0.0 124.1 jit_solution(2578316738866111626)
XLA Ops:
  1.3 2.9 %pack.1 = bf16[16,264,256]{2,1,0:T(8,128)(2,1)S(1)} custom-call(s32[1]{0:T(128)} %bitcast.1.device_ref, s32[16]{0:T(128)} %owner_ref.1, s32[16]{0:T(128)} %slot_ref.1, s32[1]{0:T(128)} %copy.15.request_ref, bf16[3,128,8192]{2,1,0:T(8,128)(2,1)} %cache_ref.1, bf16[3,3,9216]{2,1,0:T(4,128)(2,1)} %tails_ref.1), custom_call_target="tpu_custom_call" | custom-call | flops 1000 | bytes 1000 | tf_op jit(solution)/shard_map/pack/pallas_call | solution.py:79
  4.2 55.2 %all_to_all.10.held = bf16[16,264,256]{2,1,0:T(8,128)(2,1)S(1)} all-to-all(bf16[16,264,256]{2,1,0:T(8,128)(2,1)S(1)} %pack.1), channel_id=1, replica_groups=mesh['grp'=2,'req'=16] {'req'}, dimensions={0} | all-to-all | bytes 4325376 | tf_op jit(solution)/shard_map/all_to_all | solution.py:439
  59.4 1.6 %choose.1 = bf16[16,264,256]{2,1,0:T(8,128)(2,1)} custom-call(bf16[16,264,256]{2,1,0:T(8,128)(2,1)S(1)} %all_to_all.10.held), custom_call_target="tpu_custom_call" | custom-call | flops 1000 | bytes 1000 | tf_op jit(solution)/shard_map/choose/pallas_call | solution.py:112
  61.0 0.0 copy-start.3
  61.0 6.5 %all-to-all-start.1 = ((bf16[16,264,256]{2,1,0:T(8,128)(2,1)}), bf16[16,264,256]{2,1,0:T(8,128)(2,1)}, u32[]{:S(2)}, u32[]{:S(2)}) async-start(bf16[16,264,256]{2,1,0:T(8,128)(2,1)} %choose.1), calls=%async_computation.1 | async-start | bytes 4325376 | tf_op jit(solution)/shard_map/all_to_all | solution.py:440
  67.5 0.0 copy-done.3
  67.5 0.1 broadcast_in_dim.21
  67.6 0.7 broadcast_in_dim_reshape.3.skip_ref
  68.3 0.0 copy-start.4
  68.3 0.0 copy-start
  68.3 0.0 copy-start.1
  68.3 0.0 copy-start.2
  68.3 20.9 %local_part.1 = (f32[128,8192]{1,0:T(8,128)}, f32[128,8192]{1,0:T(8,128)}, bf16[128,512]{1,0:T(8,128)(2,1)}, f32[128,128]{1,0:T(8,128)}, f32[4,128,128]{2,1,0:T(8,128)}, /*index=5*/f32[8,8192]{1,0:T(8,128)}) custom-call(bf16[128,9216]{1,0:T(8,128)(2,1)} %xbc_ref.1, bf16[128,9216]{1,0:T(8,128)(2,1)} %xbc_ref.1, bf16[128,9216]{1,0:T(8,128)(2,1)} %xbc_ref.1, ...), custom_call_target="tpu_custom_call" | custom-call | flops 1000 | bytes 1000 | tf_op jit(solution)/shard_map/local_part/pallas_call | solution.py:227
  89.3 0.0 copy-done.4
  89.3 0.6 dynamic_slice.3
  90.5 0.0 copy-done
  90.5 0.0 copy-done.1
  90.5 0.0 copy-done.2
  90.5 1.0 select_maximum_fusion.channel_hbm
  91.5 24.9 %all-to-all-done.1.start_ref = bf16[16,264,256]{2,1,0:T(8,128)(2,1)} async-done(((bf16[16,264,256]{2,1,0:T(8,128)(2,1)}), bf16[16,264,256]{2,1,0:T(8,128)(2,1)}, u32[]{:S(2)}, u32[]{:S(2)}) %all-to-all-start.1) | async-done | bytes 2162720 | tf_op jit(solution)/shard_map/all_to_all | solution.py:440
  116.4 7.7 %state_part.1 = (bf16[128,8192]{1,0:T(8,128)(2,1)}, bf16[1,128,8192]{2,1,0:T(8,128)(2,1)}) custom-call(s32[1]{0:T(128)S(6)} %convert_element_type.6.live_ref, bf16[16,264,256]{2,1,0:T(8,128)(2,1)} %all-to-all-done.1.start_ref, bf16[128,9216]{1,0:T(8,128)(2,1)} %xbc_ref.1, bf16[128,512]{1,0:T(8,128)(2,1)} %get-tuple-element.8.c_hbm, ...), custom_call_target="tpu_custom_call" | custom-call | flops 402000000 | bytes 15000000 | tf_op jit(solution)/shard_map/state_part/pallas_call | solution.py:399
Async XLA Ops:
  61.0 6.5 %copy-start.3 = (f32[128]{0:T(128)S(1)}, f32[128]{0:T(128)}, u32[]{:S(2)}) copy-start(f32[128]{0:T(128)} %param.19) | copy-start | bytes 1540
  61.0 55.4 %all-to-all-start.1 = ((bf16[16,264,256]{2,1,0:T(8,128)(2,1)}), bf16[16,264,256]{2,1,0:T(8,128)(2,1)}, u32[]{:S(2)}, u32[]{:S(2)}) async-start(bf16[16,264,256]{2,1,0:T(8,128)(2,1)} %choose.1), calls=%async_computation.1 | async-start | bytes 4325376 | tf_op jit(solution)/shard_map/all_to_all | solution.py:440
  68.3 21.0 %copy-start.4 = (s32[16]{0:T(128)S(1)}, s32[16]{0:T(128)}, u32[]{:S(2)}) copy-start(s32[16]{0:T(128)} %param.24) | copy-start | bytes 196
  68.3 22.2 %copy-start = (f32[4,9216]{1,0:T(4,128)S(1)}, f32[4,9216]{1,0:T(4,128)}, u32[]{:S(2)}) copy-start(f32[4,9216]{1,0:T(4,128)} %wc_ref.1) | copy-start | bytes 442372
  68.3 22.2 %copy-start.1 = (f32[9216]{0:T(1024)S(1)}, f32[9216]{0:T(1024)}, u32[]{:S(2)}) copy-start(f32[9216]{0:T(1024)} %param.16) | copy-start | bytes 110596
  68.3 22.2 %copy-start.2 = (f32[1,8192]{1,0:T(1,128)S(1)}, f32[1,8192]{1,0:T(1,128)}, u32[]{:S(2)}) copy-start(f32[1,8192]{1,0:T(1,128)} %broadcast_in_dim_reshape.3.skip_ref) | copy-start | bytes 98308
